TPU v7x, 768 devices: a whole 4x8x12 slice. The times are simulated.
768 devices in a mesh: dp: 96 (over y_lo, z, core), pack: 8 (over x, y_hi).
Axes of the slice: x: 4, y: 8 (y_hi: 2, y_lo: 4; y = y_hi * 4 + y_lo), z: 12, core: 2. Of those that a mesh axis runs over, the one named last changes fastest.
Arguments:
- images: bfloat16 [1536, 1152], P(('dp', 'pack')), may hold values from -6 to 6
- captions: bfloat16 [3072, 1152], P(('dp', 'pack')), may hold values from -6 to 6
- caption_owner: int32 [3072], P(('dp', 'pack')), may hold values from 0 to 15, as said below
- caption_count: int32 [768], P(('dp', 'pack')), may hold values from 0 to 4, as said below
- log_scale: float32 [1], replicated, may hold values from 1.6 to 2.6
- bias: float32 [1], replicated, may hold values from -3 to 0
Outputs:
- row_loss: float32 [1536], P(('dp', 'pack'))
- grad_images: float32 [1536, 1152], P(('dp', 'pack'))
- grad_captions: float32 [3072, 1152], P(('dp', 'pack'))
Inputs may be any that keep to these rules, and one draw needn't show every extreme that they name: `caption_owner`: within each pair block, the filled slots of its 8 devices name every one of its 16 pairs exactly once; values in empty slots are arbitrary. `caption_count`: the counts of one pair block's devices sum to 16.
All inputs are finite; a program needn't handle non-finite values.
Results may differ from a plain program's by a relative error of at most 0.0043.
Values may be sent and summed in bfloat16 or wider, within the bound.
A program may use at most 32 MiB of HBM per device.

v0:
```python
import jax
import jax.numpy as jnp
from jax import lax
from jax.sharding import PartitionSpec as P

eps = 1e-06


def normalize(block_rows):
    floats = block_rows.astype(jnp.float32)
    inverse = lax.rsqrt(jnp.sum(floats * floats, axis=-1, keepdims=True) + eps)
    return (floats * inverse, inverse)


def unnormalize(unit_rows, inverse, upstream):
    return inverse * (upstream - unit_rows * jnp.sum(unit_rows * upstream, axis=-1, keepdims=True))


def body(images, captions, caption_owner, caption_count, log_scale, bias):
    pair_rows = images.shape[0]
    packers = lax.axis_size("pack")
    cycle_blocks = lax.axis_size("dp")
    group_rows = pair_rows * packers
    all_pairs = group_rows * cycle_blocks
    slot_count = captions.shape[0]
    cycle_index = lax.axis_index("dp")
    pack_index = lax.axis_index("pack")
    filled = jnp.arange(slot_count, dtype=jnp.int32) < caption_count[0]
    routing = jnp.logical_and(
        caption_owner[:, None] == jnp.arange(group_rows, dtype=jnp.int32)[None, :], filled[:, None]
    )
    outgoing = lax.dot_general(
        routing.astype(jnp.bfloat16),
        captions,
        (((0,), (0,)), ((), ())),
        preferred_element_type=jnp.float32,
    ).astype(jnp.bfloat16)
    incoming = lax.all_to_all(
        outgoing.reshape(packers, pair_rows, outgoing.shape[1]),
        "pack",
        split_axis=0,
        concat_axis=0,
        tiled=True,
    )
    owned_texts = jnp.sum(incoming.astype(jnp.float32), axis=0)
    text_unit, text_inv = normalize(owned_texts.astype(jnp.bfloat16))
    text16 = text_unit.astype(jnp.bfloat16)
    image_unit, image_inv = normalize(images)
    image16 = image_unit.astype(jnp.bfloat16)
    image_rows = lax.all_gather(image16, "pack", axis=0, tiled=True)
    logit_scale = jnp.exp(log_scale[0])
    logit_shift = bias[0]
    image_ids = cycle_index * group_rows + jnp.arange(group_rows, dtype=jnp.int32)
    column_texts = lax.all_gather(text16, "dp", axis=0, tiled=True)
    positions = jnp.arange(column_texts.shape[0], dtype=jnp.int32)
    text_ids = positions // pair_rows * group_rows + pack_index * pair_rows + positions % pair_rows
    logits = (
        logit_scale
        * lax.dot_general(
            image_rows, column_texts, (((1,), (1,)), ((), ())), preferred_element_type=jnp.float32
        )
        + logit_shift
    )
    labels = jnp.where(image_ids[:, None] == text_ids[None, :], 1.0, -1.0).astype(jnp.float32)
    losses = jnp.sum(jax.nn.softplus(-labels * logits), axis=1)
    score_weights = (-labels * jax.nn.sigmoid(-labels * logits)).astype(jnp.bfloat16)
    grad_sum = jnp.dot(score_weights, column_texts, preferred_element_type=jnp.float32)
    row_loss, grad_unit = (
        lax.psum_scatter(losses / all_pairs, "pack", scatter_dimension=0, tiled=True),
        lax.psum_scatter(logit_scale * grad_sum, "pack", scatter_dimension=0, tiled=True),
    )
    grad_images = unnormalize(image_unit, image_inv, grad_unit)
    text_grad = lax.psum_scatter(
        logit_scale
        * lax.dot_general(
            score_weights, image_rows, (((0,), (0,)), ((), ())), preferred_element_type=jnp.float32
        ),
        "dp",
        scatter_dimension=0,
        tiled=True,
    )
    owner_grad = unnormalize(text_unit, text_inv, text_grad)
    returned = lax.all_gather(owner_grad, "pack", axis=0, tiled=True)
    picked = jnp.dot(routing.astype(jnp.float32), returned, precision=lax.Precision.HIGHEST)
    return (row_loss, grad_images, picked)


def solution(mesh):
    placed = (
        P(("dp", "pack"), None),
        P(("dp", "pack"), None),
        P(("dp", "pack")),
        P(("dp", "pack")),
        P(),
        P(),
    )
    return jax.shard_map(
        body,
        mesh=mesh,
        in_specs=placed,
        out_specs=(P(("dp", "pack")), P(("dp", "pack"), None), P(("dp", "pack"), None)),
        check_vma=False,
    )
```

profile of v0, /device:TPU:1, one launch (start us, length us, event | category | flops | bytes accessed | tf_op | source)
XLA Modules:
  0.0 1086.2 jit_solution(18115192900007005937)
XLA Ops:
  7.9 0.0 copy-done
  7.9 0.6 copy-done.2
  8.5 0.3 convolution_convert_fusion
  8.8 0.6 reshape.56
  9.4 10.1 all-to-all-start
  19.5 0.0 all-reduce.6.cloned.1.call-start
  20.9 0.1 fusion.16
  21.1 0.1 fusion.19
  21.2 37.8 %all-gather = bf16[8,2,1152]{2,1,0:T(2,128)(2,1)S(1)} all-gather(bf16[1,2,1152]{2,1,0:T(2,128)(2,1)S(1)} %fusion.19), channel_id=1, replica_groups=mesh['dp'=96,'pack'=8] {'pack'}, dimensions={0}, use_global_device_ids=true | all-gather | bytes 41472 | tf_op jit(solution)/shard_map/all_gather | solution.py:50
  59.0 0.1 fusion.17
  59.1 0.1 fusion.18
  59.2 131.3 %all-gather.1 = bf16[96,2,1152]{2,1,0:T(2,128)(2,1)S(1)} all-gather(bf16[1,2,1152]{2,1,0:T(2,128)(2,1)S(1)} %fusion.18), channel_id=1, replica_groups=mesh['dp'=96,'pack'=8] {'dp'}, dimensions={0}, use_global_device_ids=true | all-gather | bytes 446976 | tf_op jit(solution)/shard_map/all_gather | solution.py:54
  190.5 0.2 reshape.60
  190.6 0.4 fusion.2
  191.0 0.9 convolution_multiply_fusion.1
  191.9 0.0 all-reduce.6.cloned.1.call-update
  191.9 0.0 all-reduce.8.cloned.1.call-start
  192.0 1.3 convolution_multiply_fusion
  193.3 0.0 all-reduce.8.cloned.1.call-update
  193.3 1.3 dynamic-slice.4
  194.6 1.3 dynamic-slice
  197.2 27.9 %all-reduce = f32[16]{0:T(128)S(1)} all-reduce(f32[16]{0:T(128)S(1)} %broadcast_multiply_fusion), channel_id=2, replica_groups=mesh['dp'=96,'pack'=8] {'pack'}, use_global_device_ids=true, to_apply=%region_4.5.clone | all-reduce | flops 16 | bytes 128
  225.1 0.6 dynamic-slice.1
  225.7 65.7 %all-reduce.6.cloned.1.call-done = f32[16,1152]{1,0:T(8,128)} async-done(((f32[16,1152]{1,0:T(8,128)}), f32[16,1152]{1,0:T(8,128)}) %all-reduce.6.cloned.1.call-update) | async-done | bytes 73744
  291.4 1.0 fusion.13
  292.3 1.4 fusion.15
  293.8 745.4 %all-reduce.8.cloned.1.call-done = f32[192,1152]{1,0:T(8,128)} async-done(((f32[192,1152]{1,0:T(8,128)}), f32[192,1152]{1,0:T(8,128)}) %all-reduce.8.cloned.1.call-update) | async-done | bytes 884752
  1039.2 1.0 fusion.9
  1040.1 0.8 fusion.12
  1041.0 37.5 %all-gather.2 = f32[8,2,1152]{2,1,0:T(2,128)S(1)} all-gather(f32[1,2,1152]{2,1,0:T(2,128)S(1)} %fusion.12), channel_id=1, replica_groups=mesh['dp'=96,'pack'=8] {'pack'}, dimensions={0}, use_global_device_ids=true | all-gather | bytes 82944 | tf_op jit(solution)/shard_map/all_gather | solution.py:83
  1078.5 0.1 reshape.62
  1078.6 0.8 fusion.23
  (13 shorter events, 0.1 us)
Async XLA Ops:
  7.2 0.7 copy-start
  7.8 0.7 copy-start.2
  9.4 49.6 %all-to-all-start = ((bf16[8,2,1152]{2,1,0:T(2,128)(2,1)}), bf16[8,2,1152]{2,1,0:T(2,128)(2,1)S(1)}, u32[]{:S(2)}, u32[]{:S(2)}) async-start(bf16[8,2,1152]{2,1,0:T(2,128)(2,1)} %reshape.56), calls=%async_computation | async-start | bytes 73728 | tf_op jit(solution)/shard_map/all_to_all | solution.py:38
  19.5 271.9 %all-reduce.6.cloned.1.call-start = ((), (), s32[]{:S(2)}) async-start(), calls=%async_computation.1 | async-start | bytes 147456
  19.6 1.4 copy-start.1
  191.9 847.2 %all-reduce.8.cloned.1.call-start = ((), (), s32[]{:S(2)}) async-start(), calls=%async_computation.2 | async-start | bytes 1769472
Sparse Core Ops, SparseCore 0:
  192.1 99.2 all-reduce.5
  294.9 744.1 all-reduce.7
where the time goes:
time: 1090 us
  waiting for transfers between devices  811 us (74%)
  blocking collectives  234 us (21%)
  between operations  17.5 us (2%)
    unnamed x4, waiting for transfers between devices  811 us
    all_gather x1, blocking collectives, body(): column_texts = lax.all_gather(text16, 'dp', axis=0, tiled=True)  131 us
    all_gather x1, blocking collectives, body(): image_rows = lax.all_gather(image16, 'pack', axis=0, tiled=True)  37.8 us
    all_gather x1, blocking collectives, body(): returned = lax.all_gather(owner_grad, 'pack', axis=0, tiled=True)  37.5 us
    unnamed x1, blocking collectives  27.9 us
  transfers between devices with their start and end apart: 3, of which 2 were waited for; matrix products, arithmetic and copies ran while one was open for 1% of the time, Pallas kernels for 0%

commit v1 on v0

v1 whole, which is shorter than its diff:
```python
import functools

import jax
import jax.numpy as jnp
from jax import lax
from jax.experimental import pallas as pl
from jax.experimental.pallas import tpu as pltpu
from jax.sharding import PartitionSpec as P

MESH = pl.DeviceIdType.MESH
EPS = 1e-06
NX, Y_HI, Y_LO, NZ = 4, 2, 4, 12
PAIR, SLOT = 2, 4
EXTRA = 128


def normalize(rows):
    inverse = lax.rsqrt(jnp.sum(rows * rows, axis=-1, keepdims=True) + EPS)
    return rows * inverse, inverse


def unnormalize(unit, inverse, upstream):
    return inverse * (upstream - unit * jnp.sum(unit * upstream, axis=-1, keepdims=True))


def softplus(v):
    return jnp.maximum(v, 0.0) + jnp.log1p(jnp.exp(-jnp.abs(v)))


def split_sum(total):
    high = total.astype(jnp.bfloat16)
    low = (total - high.astype(jnp.float32)).astype(jnp.bfloat16)
    lane = lax.broadcasted_iota(jnp.int32, (total.shape[0], EXTRA), 1)
    return jnp.where(lane == 0, high.astype(jnp.float32), jnp.where(lane == 1, low.astype(jnp.float32), 0.0))


def kernel(
    all_pairs,
    images_ref, captions_ref, owner_ref, count_ref, scale_ref, bias_ref,
    loss_ref, gi_ref, gc_ref,
    y_in, z_in, x_all, texts,
    core_out, core_in, x_out, x_in, y_out, y_back, z_out, z_back,
    send, recv,
):
    D = images_ref.shape[1]
    ny = Y_HI * Y_LO
    rows_y = PAIR * ny
    dp = lax.axis_index("dp")
    pack = lax.axis_index("pack")
    core = lax.rem(dp, 2)
    z = lax.rem(dp // 2, NZ)
    y_lo = dp // (2 * NZ)
    x = pack // Y_HI
    y_hi = lax.rem(pack, Y_HI)
    y = y_hi * Y_LO + y_lo

    def device(xx, yy, zz, cc):
        return ((lax.rem(yy, Y_LO) * NZ + zz) * 2 + cc, xx * Y_HI + yy // Y_LO)

    def at_x(k):
        return device(lax.rem(x + k + NX, NX), y, z, core)

    def at_y(k):
        return device(x, lax.rem(y + k + ny, ny), z, core)

    def at_z(k):
        return device(x, y, lax.rem(z + k + NZ, NZ), core)

    sibling = device(x, y, z, 1 - core)

    barrier = pltpu.get_barrier_semaphore()
    partners = [sibling]
    partners += [at_x(k) for k in range(1, NX)]
    partners += [at_y(k) for k in range(1, ny)]
    partners += [at_z(k) for k in range(1, NZ)]
    for partner in partners:
        pl.semaphore_signal(barrier, inc=1, device_id=partner, device_id_type=MESH)

    image_unit, image_inv = normalize(images_ref[...].astype(jnp.float32))
    y_in[0] = image_unit.astype(jnp.bfloat16)
    slot_row = lax.broadcasted_iota(jnp.int32, (SLOT, 1), 0)
    filled = slot_row < count_ref[0]
    captions = jnp.where(filled, captions_ref[...].astype(jnp.float32), 0.0)
    text_unit, text_inv = normalize(captions)
    z_in[0] = text_unit.astype(jnp.bfloat16)

    pl.semaphore_wait(barrier, len(partners))

    def copy(src, dst, sem, to):
        pltpu.make_async_remote_copy(
            src_ref=src, dst_ref=dst, send_sem=send.at[sem], recv_sem=recv.at[sem],
            device_id=to, device_id_type=MESH,
        ).start()

    def arrived(ref, sem):
        pltpu.make_async_copy(ref, ref, recv.at[sem]).wait()

    def left(ref, sem):
        pltpu.make_async_copy(ref, ref, send.at[sem]).wait()

    for k in range(1, ny):
        copy(y_in.at[0], y_in.at[k], 0, at_y(k))
    for k in range(1, NZ):
        copy(z_in.at[0], z_in.at[k], 1, at_z(k))

    arrived(y_in.at[pl.ds(1, ny - 1)], 0)
    x_all[0, 0] = jnp.concatenate([y_in[k].astype(jnp.float32) for k in range(ny)], axis=0).astype(jnp.bfloat16)
    for k in range(1, NX):
        copy(x_all.at[0, 0], x_all.at[0, k], 2, at_x(k))
    copy(x_all.at[0, 0], x_all.at[1, 0], 3, sibling)

    arrived(z_in.at[pl.ds(1, NZ - 1)], 1)
    texts[...] = jnp.concatenate([z_in[k].astype(jnp.float32) for k in range(NZ)], axis=0).astype(jnp.bfloat16)

    arrived(x_all.at[0, pl.ds(1, NX - 1)], 2)
    copy(x_all.at[0, pl.ds(1, NX - 1)], x_all.at[1, pl.ds(1, NX - 1)], 4, sibling)

    rows = NX * rows_y
    own = lax.broadcasted_iota(jnp.int32, (2 * rows, NZ * SLOT), 0)
    column = lax.broadcasted_iota(jnp.int32, (2 * rows, NZ * SLOT), 1)
    from_x = lax.rem(x - lax.rem(own // rows_y, NX) + NX, NX)
    y_slot = lax.rem(own, rows_y) // PAIR
    from_y_hi = lax.rem(y_hi - y_slot // Y_LO + Y_HI, Y_HI)
    pair = (from_x * Y_HI + from_y_hi) * PAIR + lax.rem(own, PAIR)
    pair = jnp.where(jnp.logical_and(own < rows, lax.rem(y_slot, Y_LO) == 0), pair, -1)
    owner = jnp.full_like(column, -2)
    for s in range(SLOT):
        owner = jnp.where(jnp.logical_and(column == s, s < count_ref[0]), owner_ref[s], owner)
    sign = jnp.where(pair == owner, -1.0, 1.0)

    scale = jnp.exp(jnp.full((1, 1), scale_ref[0], jnp.float32))
    bias = jnp.full((1, 1), bias_ref[0], jnp.float32)

    arrived(x_all.at[1, 0], 3)
    arrived(x_all.at[1, pl.ds(1, NX - 1)], 4)

    image_rows = x_all[...].reshape(2 * rows, D)
    text_rows = texts[...]
    dots = lax.dot_general(image_rows, text_rows, (((1,), (1,)), ((), ())), preferred_element_type=jnp.float32)
    v = sign * (scale * dots + bias)
    small = jnp.exp(-jnp.abs(v))
    losses = jnp.sum(jnp.maximum(v, 0.0) + jnp.log1p(small), axis=1, keepdims=True)
    weights = (sign * jnp.where(v >= 0.0, 1.0, small) / (1.0 + small)).astype(jnp.bfloat16)

    core_out[:, :D] = (scale * jnp.dot(weights[rows:], text_rows, preferred_element_type=jnp.float32)).astype(jnp.bfloat16)
    core_out[:, D:] = split_sum(losses[rows:]).astype(jnp.bfloat16)
    copy(core_out, core_in, 5, sibling)

    text_grad = scale * lax.dot_general(weights, image_rows, (((0,), (0,)), ((), ())), preferred_element_type=jnp.float32)
    for k in range(1, NZ):
        z_out[k] = text_grad[k * SLOT:(k + 1) * SLOT].astype(jnp.bfloat16)
        copy(z_out.at[k], z_back.at[k], 6, at_z(-k))

    mine = scale * jnp.dot(weights[:rows], text_rows, preferred_element_type=jnp.float32)
    arrived(core_in, 5)
    mine = mine + core_in[:, :D].astype(jnp.float32)
    other = core_in[:, D:].astype(jnp.float32)
    loss = losses[:rows] + jnp.sum(other, axis=1, keepdims=True)
    for k in range(1, NX):
        part = slice(k * rows_y, (k + 1) * rows_y)
        x_out[k, :, :D] = mine[part].astype(jnp.bfloat16)
        x_out[k, :, D:] = split_sum(loss[part]).astype(jnp.bfloat16)
        copy(x_out.at[k], x_in.at[k], 7, at_x(-k))
    mine, loss = mine[:rows_y], loss[:rows_y]

    arrived(x_in.at[pl.ds(1, NX - 1)], 7)
    for k in range(1, NX):
        mine = mine + x_in[k, :, :D].astype(jnp.float32)
        loss = loss + jnp.sum(x_in[k, :, D:].astype(jnp.float32), axis=1, keepdims=True)
    pieces = split_sum(loss)
    for k in range(1, ny):
        part = slice(k * PAIR, (k + 1) * PAIR)
        y_out[k, :, :D] = mine[part].astype(jnp.bfloat16)
        y_out[k, :, D:] = pieces[part].astype(jnp.bfloat16)
        copy(y_out.at[k], y_back.at[k], 8, at_y(-k))
    mine, loss = mine[:PAIR], loss[:PAIR]

    text_mine = text_grad[:SLOT]
    arrived(z_back.at[pl.ds(1, NZ - 1)], 6)
    for k in range(1, NZ):
        text_mine = text_mine + z_back[k].astype(jnp.float32)
    gc_ref[...] = jnp.where(filled, unnormalize(text_unit, text_inv, text_mine), 0.0)

    arrived(y_back.at[pl.ds(1, ny - 1)], 8)
    for k in range(1, ny):
        mine = mine + y_back[k, :, :D].astype(jnp.float32)
        loss = loss + jnp.sum(y_back[k, :, D:].astype(jnp.float32), axis=1, keepdims=True)
    gi_ref[...] = unnormalize(image_unit, image_inv, mine)
    loss_ref[...] = jnp.broadcast_to(loss / all_pairs - softplus(bias), loss_ref.shape)

    left(y_in.at[pl.ds(1, ny - 1)], 0)
    left(z_in.at[pl.ds(1, NZ - 1)], 1)
    left(x_all.at[0, pl.ds(1, NX - 1)], 2)
    left(x_all.at[1, 0], 3)
    left(x_all.at[1, pl.ds(1, NX - 1)], 4)
    left(core_out, 5)
    left(z_out.at[pl.ds(1, NZ - 1)], 6)
    left(x_out.at[pl.ds(1, NX - 1)], 7)
    left(y_out.at[pl.ds(1, ny - 1)], 8)


def body(images, captions, caption_owner, caption_count, log_scale, bias):
    D = images.shape[1]
    W = D + EXTRA
    ny = Y_HI * Y_LO
    rows_y = PAIR * ny
    rows = NX * rows_y
    all_pairs = PAIR * 2 * NX * ny * NZ
    vmem = pl.BlockSpec(memory_space=pltpu.VMEM)
    smem = pl.BlockSpec(memory_space=pltpu.SMEM)
    half = jnp.bfloat16
    loss, gi, gc = pl.pallas_call(
        functools.partial(kernel, all_pairs),
        out_shape=(
            jax.ShapeDtypeStruct((PAIR, 128), jnp.float32),
            jax.ShapeDtypeStruct((PAIR, D), jnp.float32),
            jax.ShapeDtypeStruct((SLOT, D), jnp.float32),
        ),
        in_specs=[vmem, vmem, smem, smem, smem, smem],
        out_specs=(vmem, vmem, vmem),
        scratch_shapes=[
            pltpu.VMEM((ny, PAIR, D), half),
            pltpu.VMEM((NZ, SLOT, D), half),
            pltpu.VMEM((2, NX, rows_y, D), half),
            pltpu.VMEM((NZ * SLOT, D), half),
            pltpu.VMEM((rows, W), half),
            pltpu.VMEM((rows, W), half),
            pltpu.VMEM((NX, rows_y, W), half),
            pltpu.VMEM((NX, rows_y, W), half),
            pltpu.VMEM((ny, PAIR, W), half),
            pltpu.VMEM((ny, PAIR, W), half),
            pltpu.VMEM((NZ, SLOT, D), half),
            pltpu.VMEM((NZ, SLOT, D), half),
            pltpu.SemaphoreType.DMA((9,)),
            pltpu.SemaphoreType.DMA((9,)),
        ],
        compiler_params=pltpu.CompilerParams(
            collective_id=0, has_side_effects=True, vmem_limit_bytes=32 * 1024 * 1024
        ),
    )(images, captions, caption_owner, caption_count, log_scale, bias)
    return loss[:, 0], gi, gc


def solution(mesh):
    placed = (
        P(("dp", "pack"), None),
        P(("dp", "pack"), None),
        P(("dp", "pack")),
        P(("dp", "pack")),
        P(),
        P(),
    )
    return jax.shard_map(
        body,
        mesh=mesh,
        in_specs=placed,
        out_specs=(P(("dp", "pack")), P(("dp", "pack"), None), P(("dp", "pack"), None)),
        check_vma=False,
    )
```

time: 1090 us -> 44.2 us (0.04)
  waiting for transfers between devices: 811 us -> 0 us
  blocking collectives: 234 us -> 0 us
  Pallas kernels: 0 us -> 38.8 us
  between operations: 17.5 us -> 2.64 us
    unnamed x4 -> x0, waiting for transfers between devices: 811 us -> none
    all_gather x3 -> x0, blocking collectives: 207 us -> none  [the longest x1 131 us: body(): column_texts = lax.all_gather(text16, 'dp', axis=0, tiled=True)]
    pallas_call x0 -> x1, Pallas kernels: none -> 38.8 us  [body(): pl.pallas_call(functools.partial(kernel, all_pairs), out_shape=(jax.Shape...]
    unnamed x1 -> x0, blocking collectives: 27.9 us -> none
  transfers between devices with their start and end apart: 3 -> 0, of which waited for: 2 -> 0; matrix products, arithmetic and copies ran while one was open for 1% -> 0% of each run, Pallas kernels for 0% -> 0%
where the time goes in v1:
time: 44.2 us; the launch traced here: 43.9 us
  Pallas kernels  38.8 us (88%)
  between operations  2.64 us (6%)
  local copies, waits for them, and re-layouts  2.53 us (6%)
    pallas_call x1, Pallas kernels, body(): pl.pallas_call(functools.partial(kernel, all_pairs), out_shape=(jax.Shape...  38.8 us
    unnamed x8, local copies, waits for them, and re-layouts  1.9 us

profile of v1, /device:TPU:1, one launch (start us, length us, event | category | flops | bytes accessed | tf_op | source)
XLA Modules:
  0.0 43.9 jit_solution(14665580452196916694)
XLA Ops:
  0.6 0.0 copy-start.1
  1.9 0.0 copy-start.2
  2.6 0.0 copy-done.1
  2.6 0.0 copy-done.2
  2.6 0.0 copy-start
  2.6 0.7 %copy-done = bf16[4,1152]{1,0:T(4,128)(2,1)S(1)} copy-done((bf16[4,1152]{1,0:T(4,128)(2,1)S(1)}, bf16[4,1152]{1,0:T(4,128)(2,1)}, u32[]{:S(2)}) %copy-start) | copy-done | bytes 9240
  3.3 38.8 %shard_map.85 = (f32[2,128]{1,0:T(2,128)S(1)}, f32[2,1152]{1,0:T(2,128)S(1)}, f32[4,1152]{1,0:T(4,128)S(1)}) custom-call(bf16[2,1152]{1,0:T(2,128)(2,1)S(1)} %copy-done.1, bf16[4,1152]{1,0:T(4,128)(2,1)S(1)} %copy-done, s32[4]{0:T(128)S(1)} %copy-done.2, s32[1]{0:T(128)S(6)} %copy.11.count_ref, f32[1]{0:T(128)S(6)} %copy.12.scale_ref, f32[1]{0:T(128)S(6)} %copy.13.bias_ref), custom_call_target="tpu_custom_call" | custom-call | tf_op jit(solution)/shard_map/pallas_call | solution.py:212
  42.1 0.6 %slice_reduce_fusion = f32[2]{0:T(128)} fusion(f32[2,128]{1,0:T(2,128)S(1)} %get-tuple-element.6), kind=kLoop, calls=%fused_computation | loop fusion | bytes 16 | tf_op jit(solution)/shard_map/slice | solution.py:241
  42.7 0.6 %copy.14 = f32[2,1152]{1,0:T(2,128)} copy(f32[2,1152]{1,0:T(2,128)S(1)} %get-tuple-element.13) | data formatting | bytes 18432
  43.3 0.6 %copy.15 = f32[4,1152]{1,0:T(4,128)} copy(f32[4,1152]{1,0:T(4,128)S(1)} %get-tuple-element.14) | data formatting | bytes 36864
Async XLA Ops:
  0.6 2.0 %copy-start.1 = (bf16[2,1152]{1,0:T(2,128)(2,1)S(1)}, bf16[2,1152]{1,0:T(2,128)(2,1)}, u32[]{:S(2)}) copy-start(bf16[2,1152]{1,0:T(2,128)(2,1)} %images_ref.1) | copy-start | bytes 13828
  1.9 0.7 %copy-start.2 = (s32[4]{0:T(128)S(1)}, s32[4]{0:T(128)}, u32[]{:S(2)}) copy-start(s32[4]{0:T(128)} %owner_ref.1) | copy-start | bytes 52
  2.6 0.7 %copy-start = (bf16[4,1152]{1,0:T(4,128)(2,1)S(1)}, bf16[4,1152]{1,0:T(4,128)(2,1)}, u32[]{:S(2)}) copy-start(bf16[4,1152]{1,0:T(4,128)(2,1)} %captions_ref.1) | copy-start | bytes 27652

commit v2 on v1

v2 whole, which is shorter than its diff:
```python
import functools

import jax
import jax.numpy as jnp
from jax import lax
from jax.experimental import pallas as pl
from jax.experimental.pallas import tpu as pltpu
from jax.sharding import PartitionSpec as P

MESH = pl.DeviceIdType.MESH
EPS = 1e-06
NX, Y_HI, Y_LO, NZ = 4, 2, 4, 12
PAIR, SLOT = 2, 4
EXTRA = 128


def normalize(rows):
    inverse = lax.rsqrt(jnp.sum(rows * rows, axis=-1, keepdims=True) + EPS)
    return rows * inverse, inverse


def unnormalize(unit, inverse, upstream):
    return inverse * (upstream - unit * jnp.sum(unit * upstream, axis=-1, keepdims=True))


def softplus(v):
    return jnp.maximum(v, 0.0) + jnp.log1p(jnp.exp(-jnp.abs(v)))


def split_sum(total):
    high = total.astype(jnp.bfloat16)
    low = (total - high.astype(jnp.float32)).astype(jnp.bfloat16)
    lane = lax.broadcasted_iota(jnp.int32, (total.shape[0], EXTRA), 1)
    return jnp.where(lane == 0, high.astype(jnp.float32), jnp.where(lane == 1, low.astype(jnp.float32), 0.0))


def kernel(
    all_pairs,
    images_hbm, captions_hbm, owner_hbm, count_ref, scale_ref, bias_ref,
    loss_ref, gi_ref, gc_ref,
    images_ref, captions_ref, owner_ref,
    xy_in, z_in, x_all, texts,
    core_out, core_in, xy_out, xy_back, z_out, z_back,
    load, send, recv,
):
    D = images_ref.shape[1]
    ny = Y_HI * Y_LO
    nxy = NX * ny
    rows = PAIR * nxy
    loads = [
        pltpu.make_async_copy(src, dst, load.at[i])
        for i, (src, dst) in enumerate((
            (images_hbm, images_ref), (captions_hbm, captions_ref), (owner_hbm, owner_ref),
        ))
    ]
    for one in loads:
        one.start()
    dp = lax.axis_index("dp")
    pack = lax.axis_index("pack")
    core = lax.rem(dp, 2)
    z = lax.rem(dp // 2, NZ)
    y_lo = dp // (2 * NZ)
    x = pack // Y_HI
    y_hi = lax.rem(pack, Y_HI)
    y = y_hi * Y_LO + y_lo

    def device(xx, yy, zz, cc):
        return ((lax.rem(yy, Y_LO) * NZ + zz) * 2 + cc, xx * Y_HI + yy // Y_LO)

    def at_xy(k, way):
        kx, ky = k % NX, k // NX
        return device(lax.rem(x + way * kx + NX, NX), lax.rem(y + way * ky + ny, ny), z, core)

    def at_z(k):
        return device(x, y, lax.rem(z + k + NZ, NZ), core)

    sibling = device(x, y, z, 1 - core)

    def hops(k, n):
        return min(k, n - k)

    far_xy = sorted(range(1, nxy), key=lambda k: -hops(k % NX, NX) - hops(k // NX, ny))
    far_z = sorted(range(1, NZ), key=lambda k: -hops(k, NZ))

    barrier = pltpu.get_barrier_semaphore()
    partners = [sibling]
    partners += [at_z(k) for k in far_z]
    partners += [at_xy(k, 1) for k in far_xy]
    for partner in partners:
        pl.semaphore_signal(barrier, inc=1, device_id=partner, device_id_type=MESH)

    loads[0].wait()
    image_unit, image_inv = normalize(images_ref[...].astype(jnp.float32))
    xy_in[0] = image_unit.astype(jnp.bfloat16)
    loads[1].wait()
    slot_row = lax.broadcasted_iota(jnp.int32, (SLOT, 1), 0)
    filled = slot_row < count_ref[0]
    captions = jnp.where(filled, captions_ref[...].astype(jnp.float32), 0.0)
    text_unit, text_inv = normalize(captions)
    z_in[0] = text_unit.astype(jnp.bfloat16)

    pl.semaphore_wait(barrier, len(partners))

    sent = []

    def copy(src, dst, sem, to):
        pltpu.make_async_remote_copy(
            src_ref=src, dst_ref=dst, send_sem=send.at[sem], recv_sem=recv.at[sem],
            device_id=to, device_id_type=MESH,
        ).start()

    def arrived(ref, sem):
        pltpu.make_async_copy(ref, ref, recv.at[sem]).wait()

    for k in far_z:
        copy(z_in.at[0], z_in.at[k], 1, at_z(k))
    sent.append((z_in.at[pl.ds(1, NZ - 1)], 1))
    for k in far_xy:
        copy(xy_in.at[0], xy_in.at[k], 0, at_xy(k, 1))
    sent.append((xy_in.at[pl.ds(1, nxy - 1)], 0))

    arrived(xy_in.at[pl.ds(1, nxy - 1)], 0)
    x_all[0] = jnp.concatenate([xy_in[k].astype(jnp.float32) for k in range(nxy)], axis=0).astype(jnp.bfloat16)
    copy(x_all.at[0], x_all.at[1], 3, sibling)
    sent.append((x_all.at[1], 3))

    arrived(z_in.at[pl.ds(1, NZ - 1)], 1)
    texts[...] = jnp.concatenate([z_in[k].astype(jnp.float32) for k in range(NZ)], axis=0).astype(jnp.bfloat16)

    loads[2].wait()
    own = lax.broadcasted_iota(jnp.int32, (2 * rows, NZ * SLOT), 0)
    column = lax.broadcasted_iota(jnp.int32, (2 * rows, NZ * SLOT), 1)
    slot = lax.rem(own, rows) // PAIR
    y_slot = slot // NX
    from_x = lax.rem(x - lax.rem(slot, NX) + NX, NX)
    from_y_hi = lax.rem(y_hi - y_slot // Y_LO + Y_HI, Y_HI)
    pair = (from_x * Y_HI + from_y_hi) * PAIR + lax.rem(own, PAIR)
    pair = jnp.where(jnp.logical_and(own < rows, lax.rem(y_slot, Y_LO) == 0), pair, -1)
    owner = jnp.full_like(column, -2)
    for s in range(SLOT):
        owner = jnp.where(jnp.logical_and(column == s, s < count_ref[0]), owner_ref[s], owner)
    sign = jnp.where(pair == owner, -1.0, 1.0)

    scale = jnp.exp(jnp.full((1, 1), scale_ref[0], jnp.float32))
    bias = jnp.full((1, 1), bias_ref[0], jnp.float32)

    arrived(x_all.at[1], 3)

    image_rows = x_all[...].reshape(2 * rows, D)
    text_rows = texts[...]
    dots = lax.dot_general(image_rows, text_rows, (((1,), (1,)), ((), ())), preferred_element_type=jnp.float32)
    v = sign * (scale * dots + bias)
    small = jnp.exp(-jnp.abs(v))
    losses = jnp.sum(jnp.maximum(v, 0.0) + jnp.log1p(small), axis=1, keepdims=True)
    weights = (sign * jnp.where(v >= 0.0, 1.0, small) / (1.0 + small)).astype(jnp.bfloat16)

    core_out[:, :D] = (scale * jnp.dot(weights[rows:], text_rows, preferred_element_type=jnp.float32)).astype(jnp.bfloat16)
    core_out[:, D:] = split_sum(losses[rows:]).astype(jnp.bfloat16)
    copy(core_out, core_in, 5, sibling)
    sent.append((core_out, 5))

    text_grad = scale * lax.dot_general(weights, image_rows, (((0,), (0,)), ((), ())), preferred_element_type=jnp.float32)
    for k in far_z:
        z_out[k] = text_grad[k * SLOT:(k + 1) * SLOT].astype(jnp.bfloat16)
        copy(z_out.at[k], z_back.at[k], 6, at_z(-k))
    sent.append((z_out.at[pl.ds(1, NZ - 1)], 6))

    mine = scale * jnp.dot(weights[:rows], text_rows, preferred_element_type=jnp.float32)
    arrived(core_in, 5)
    mine = mine + core_in[:, :D].astype(jnp.float32)
    other = core_in[:, D:].astype(jnp.float32)
    loss = losses[:rows] + jnp.sum(other, axis=1, keepdims=True)
    pieces = split_sum(loss)
    for k in far_xy:
        part = slice(k * PAIR, (k + 1) * PAIR)
        xy_out[k, :, :D] = mine[part].astype(jnp.bfloat16)
        xy_out[k, :, D:] = pieces[part].astype(jnp.bfloat16)
        copy(xy_out.at[k], xy_back.at[k], 7, at_xy(k, -1))
    sent.append((xy_out.at[pl.ds(1, nxy - 1)], 7))
    mine, loss = mine[:PAIR], loss[:PAIR]

    text_mine = text_grad[:SLOT]
    arrived(z_back.at[pl.ds(1, NZ - 1)], 6)
    for k in range(1, NZ):
        text_mine = text_mine + z_back[k].astype(jnp.float32)
    gc_ref[...] = jnp.where(filled, unnormalize(text_unit, text_inv, text_mine), 0.0)

    arrived(xy_back.at[pl.ds(1, nxy - 1)], 7)
    for k in range(1, nxy):
        mine = mine + xy_back[k, :, :D].astype(jnp.float32)
        loss = loss + jnp.sum(xy_back[k, :, D:].astype(jnp.float32), axis=1, keepdims=True)
    gi_ref[...] = unnormalize(image_unit, image_inv, mine)
    loss_ref[...] = (loss / all_pairs - softplus(bias))[:, 0]

    for ref, sem in sent:
        pltpu.make_async_copy(ref, ref, send.at[sem]).wait()


def hand_over(loss_in, gi_in, gc_in, loss_ref, gi_ref, gc_ref):
    loss_ref[...] = loss_in[...]
    gi_ref[...] = gi_in[...]
    gc_ref[...] = gc_in[...]


def body(images, captions, caption_owner, caption_count, log_scale, bias):
    D = images.shape[1]
    W = D + EXTRA
    ny = Y_HI * Y_LO
    nxy = NX * ny
    rows = PAIR * nxy
    all_pairs = PAIR * 2 * NX * ny * NZ
    vmem = pl.BlockSpec(memory_space=pltpu.VMEM)
    half = jnp.bfloat16
    loss, gi, gc = pl.pallas_call(
        functools.partial(kernel, all_pairs),
        out_shape=(
            jax.ShapeDtypeStruct((PAIR,), jnp.float32),
            jax.ShapeDtypeStruct((PAIR, D), jnp.float32),
            jax.ShapeDtypeStruct((SLOT, D), jnp.float32),
        ),
        in_specs=[pl.BlockSpec(memory_space=pltpu.HBM)] * 3 + [pl.BlockSpec(memory_space=pltpu.SMEM)] * 3,
        out_specs=(vmem, vmem, vmem),
        scratch_shapes=[
            pltpu.VMEM((PAIR, D), half),
            pltpu.VMEM((SLOT, D), half),
            pltpu.SMEM((SLOT,), jnp.int32),
            pltpu.VMEM((nxy, PAIR, D), half),
            pltpu.VMEM((NZ, SLOT, D), half),
            pltpu.VMEM((2, rows, D), half),
            pltpu.VMEM((NZ * SLOT, D), half),
            pltpu.VMEM((rows, W), half),
            pltpu.VMEM((rows, W), half),
            pltpu.VMEM((nxy, PAIR, W), half),
            pltpu.VMEM((nxy, PAIR, W), half),
            pltpu.VMEM((NZ, SLOT, D), half),
            pltpu.VMEM((NZ, SLOT, D), half),
            pltpu.SemaphoreType.DMA((3,)),
            pltpu.SemaphoreType.DMA((9,)),
            pltpu.SemaphoreType.DMA((9,)),
        ],
        compiler_params=pltpu.CompilerParams(
            collective_id=0, has_side_effects=True, vmem_limit_bytes=32 * 1024 * 1024
        ),
    )(
        *[pltpu.with_memory_space_constraint(a, pltpu.HBM) for a in (images, captions, caption_owner)],
        caption_count, log_scale, bias,
    )
    loss, gi, gc = pl.pallas_call(
        hand_over,
        out_shape=(
            jax.ShapeDtypeStruct((PAIR,), jnp.float32),
            jax.ShapeDtypeStruct((PAIR, D), jnp.float32),
            jax.ShapeDtypeStruct((SLOT, D), jnp.float32),
        ),
        in_specs=[vmem] * 3,
        out_specs=(vmem, vmem, vmem),
    )(loss, gi, gc)
    return loss, gi, gc


def solution(mesh):
    placed = (
        P(("dp", "pack"), None),
        P(("dp", "pack"), None),
        P(("dp", "pack")),
        P(("dp", "pack")),
        P(),
        P(),
    )
    return jax.shard_map(
        body,
        mesh=mesh,
        in_specs=placed,
        out_specs=(P(("dp", "pack")), P(("dp", "pack"), None), P(("dp", "pack"), None)),
        check_vma=False,
    )
```

time: 44.2 us -> 41.3 us (0.934)
  Pallas kernels: 38.8 us -> 36.7 us
  local copies, waits for them, and re-layouts: 2.53 us -> 1.77 us
    pallas_call x1, Pallas kernels: 38.8 us -> 35.4 us  [body(): pl.pallas_call(functools.partial(kernel, all_pairs), out_shape=(jax.Shape...]
    pallas_call x0 -> x1, Pallas kernels: none -> 1.36 us  [body(): pl.pallas_call(hand_over, out_shape=(jax.ShapeDtypeStruct((PAIR,), jnp.fl...]
    slice x1 -> x0, local copies, waits for them, and re-layouts: 0.63 us -> none  [body(): return (loss[:, 0], gi, gc)]
    unnamed x8 -> x6, local copies, waits for them, and re-layouts: 1.9 us -> 1.77 us
where the time goes in v2:
time: 41.3 us; the launch traced here: 41.1 us
  Pallas kernels  36.7 us (89%)
  between operations  2.59 us (6%)
  local copies, waits for them, and re-layouts  1.77 us (4%)
    pallas_call x1, Pallas kernels, body(): pl.pallas_call(functools.partial(kernel, all_pairs), out_shape=(jax.Shape...  35.4 us
    unnamed x6, local copies, waits for them, and re-layouts  1.77 us
    pallas_call x1, Pallas kernels, body(): pl.pallas_call(hand_over, out_shape=(jax.ShapeDtypeStruct((PAIR,), jnp.fl...  1.36 us

profile of v2, /device:TPU:1, one launch (start us, length us, event | category | flops | bytes accessed | tf_op | source)
XLA Modules:
  0.0 41.1 jit_solution(6275267655835172653)
XLA Ops:
  2.6 35.4 %shard_map.85 = (f32[2]{0:T(128)S(1)}, f32[2,1152]{1,0:T(2,128)S(1)}, f32[4,1152]{1,0:T(4,128)S(1)}) custom-call(bf16[2,1152]{1,0:T(2,128)(2,1)} %images_hbm.1, bf16[4,1152]{1,0:T(4,128)(2,1)} %captions_hbm.1, s32[4]{0:T(128)} %owner_hbm.1, s32[1]{0:T(128)S(6)} %copy.9.count_ref, f32[1]{0:T(128)S(6)} %copy.10.scale_ref, f32[1]{0:T(128)S(6)} %copy.11.bias_ref), custom_call_target="tpu_custom_call" | custom-call | tf_op jit(solution)/shard_map/pallas_call | solution.py:214
  37.9 0.0 copy-start
  37.9 0.6 %copy-done = f32[4,1152]{1,0:T(4,128)} copy-done((f32[4,1152]{1,0:T(4,128)}, f32[4,1152]{1,0:T(4,128)S(1)}, u32[]{:S(2)}) %copy-start) | copy-done | bytes 18456
  38.5 0.0 copy-start.1
  38.5 0.6 %copy-done.1 = f32[2,1152]{1,0:T(2,128)} copy-done((f32[2,1152]{1,0:T(2,128)}, f32[2,1152]{1,0:T(2,128)S(1)}, u32[]{:S(2)}) %copy-start.1) | copy-done | bytes 9240
  39.1 0.0 copy-start.2
  39.1 0.6 %copy-done.2 = f32[2]{0:T(128)} copy-done((f32[2]{0:T(128)}, f32[2]{0:T(128)S(1)}, u32[]{:S(2)}) %copy-start.2) | copy-done | bytes 32
  39.7 1.4 %shard_map.86 = (f32[2]{0:T(128)}, f32[2,1152]{1,0:T(2,128)}, f32[4,1152]{1,0:T(4,128)}) custom-call(f32[2]{0:T(128)} %copy-done.2, f32[2,1152]{1,0:T(2,128)} %copy-done.1, f32[4,1152]{1,0:T(4,128)} %copy-done), custom_call_target="tpu_custom_call" | custom-call | tf_op jit(solution)/shard_map/pallas_call | solution.py:248
Async XLA Ops:
  37.9 0.6 %copy-start = (f32[4,1152]{1,0:T(4,128)}, f32[4,1152]{1,0:T(4,128)S(1)}, u32[]{:S(2)}) copy-start(f32[4,1152]{1,0:T(4,128)S(1)} %get-tuple-element.8.gc_in) | copy-start | bytes 55300
  38.5 0.6 %copy-start.1 = (f32[2,1152]{1,0:T(2,128)}, f32[2,1152]{1,0:T(2,128)S(1)}, u32[]{:S(2)}) copy-start(f32[2,1152]{1,0:T(2,128)S(1)} %get-tuple-element.7.gi_in) | copy-start | bytes 27652
  39.1 0.6 %copy-start.2 = (f32[2]{0:T(128)}, f32[2]{0:T(128)S(1)}, u32[]{:S(2)}) copy-start(f32[2]{0:T(128)S(1)} %get-tuple-element.6.loss_in) | copy-start | bytes 28

commit v3 on v2

v3 whole, which is shorter than its diff:
```python
import functools

import jax
import jax.numpy as jnp
from jax import lax
from jax.experimental import pallas as pl
from jax.experimental.pallas import tpu as pltpu
from jax.sharding import PartitionSpec as P

MESH = pl.DeviceIdType.MESH
EPS = 1e-06
NX, Y_HI, Y_LO, NZ = 4, 2, 4, 12
PAIR, SLOT = 2, 4
EXTRA = 128


def normalize(rows):
    inverse = lax.rsqrt(jnp.sum(rows * rows, axis=-1, keepdims=True) + EPS)
    return rows * inverse, inverse


def unnormalize(unit, inverse, upstream):
    return inverse * (upstream - unit * jnp.sum(unit * upstream, axis=-1, keepdims=True))


def softplus(v):
    return jnp.maximum(v, 0.0) + jnp.log1p(jnp.exp(-jnp.abs(v)))


def split_sum(total):
    high = total.astype(jnp.bfloat16)
    low = (total - high.astype(jnp.float32)).astype(jnp.bfloat16)
    lane = lax.broadcasted_iota(jnp.int32, (total.shape[0], EXTRA), 1)
    return jnp.where(lane == 0, high.astype(jnp.float32), jnp.where(lane == 1, low.astype(jnp.float32), 0.0))


def kernel(
    all_pairs,
    images_hbm, captions_hbm, owner_hbm, count_ref, scale_ref, bias_ref,
    loss_ref, gi_ref, gc_ref,
    images_ref, captions_ref, owner_ref,
    xy_in, z_in, core_out, core_in, xy_out, xy_back, z_out, z_back,
    load, send, recv,
):
    D = images_ref.shape[1]
    ny = Y_HI * Y_LO
    nxy = NX * ny
    rows = PAIR * nxy
    columns = SLOT * NZ
    dp = lax.axis_index("dp")
    pack = lax.axis_index("pack")
    core = lax.rem(dp, 2)
    z = lax.rem(dp // 2, NZ)
    y_lo = dp // (2 * NZ)
    x = pack // Y_HI
    y_hi = lax.rem(pack, Y_HI)
    y = y_hi * Y_LO + y_lo

    def device(xx, yy, zz, cc):
        return ((lax.rem(yy, Y_LO) * NZ + zz) * 2 + cc, xx * Y_HI + yy // Y_LO)

    def at_xy(k, way, cc):
        kx, ky = k % NX, k // NX
        return device(lax.rem(x + way * kx + NX, NX), lax.rem(y + way * ky + ny, ny), z, cc)

    def at_z(k):
        return device(x, y, lax.rem(z + k + NZ, NZ), core)

    def hops(k, n):
        return min(k, n - k)

    other = 1 - core
    sibling = device(x, y, z, other)
    order = sorted(range(nxy), key=lambda k: hops(k % NX, NX) + hops(k // NX, ny))
    last = nxy - 1
    far = order[last]
    near = pl.ds(1, nxy - 2)
    far_z = sorted(range(1, NZ), key=lambda k: -hops(k, NZ))

    loads = [
        pltpu.make_async_copy(src, dst, load.at[i])
        for i, (src, dst) in enumerate((
            (images_hbm, images_ref), (captions_hbm, captions_ref), (owner_hbm, owner_ref),
        ))
    ]
    for one in loads:
        one.start()
    barrier = pltpu.get_barrier_semaphore()
    partners = [at_xy(far, 1, core), at_xy(far, 1, other)]
    partners += [at_z(k) for k in far_z]
    partners += [at_xy(order[p], 1, core) for p in range(last - 1, 0, -1)]
    partners += [sibling]
    for partner in partners:
        pl.semaphore_signal(barrier, inc=1, device_id=partner, device_id_type=MESH)

    loads[0].wait()
    image_unit, image_inv = normalize(images_ref[...].astype(jnp.float32))
    xy_in[0, 0] = image_unit.astype(jnp.bfloat16)
    loads[1].wait()
    slot_row = lax.broadcasted_iota(jnp.int32, (SLOT, 1), 0)
    filled = slot_row < count_ref[0]
    captions = jnp.where(filled, captions_ref[...].astype(jnp.float32), 0.0)
    text_unit, text_inv = normalize(captions)
    z_in[0] = text_unit.astype(jnp.bfloat16)
    loads[2].wait()

    own = lax.broadcasted_iota(jnp.int32, (rows, columns), 0)
    column = lax.broadcasted_iota(jnp.int32, (rows, columns), 1)
    pair = jnp.full_like(own, -1)
    for p, k in enumerate(order):
        kx, ky = k % NX, k // NX
        if ky % Y_LO == 0:
            first = lax.rem(x - kx + NX, NX) * Y_HI + lax.rem(y_hi - ky // Y_LO + Y_HI, Y_HI)
            pair = jnp.where(own // PAIR == p, first * PAIR + lax.rem(own, PAIR), pair)
    owner = jnp.full_like(column, -2)
    for s in range(SLOT):
        owner = jnp.where(jnp.logical_and(column == s, s < count_ref[0]), owner_ref[s], owner)
    sign = jnp.where(pair == owner, -1.0, 1.0)
    scale = jnp.exp(jnp.full((1, 1), scale_ref[0], jnp.float32))
    bias = jnp.full((1, 1), bias_ref[0], jnp.float32)

    pl.semaphore_wait(barrier, len(partners))

    sent = []

    def copy(src, dst, sem, to):
        pltpu.make_async_remote_copy(
            src_ref=src, dst_ref=dst, send_sem=send.at[sem], recv_sem=recv.at[sem],
            device_id=to, device_id_type=MESH,
        ).start()

    def arrived(ref, sem):
        pltpu.make_async_copy(ref, ref, recv.at[sem]).wait()

    copy(xy_in.at[0, 0], xy_in.at[1, last], 9, at_xy(far, 1, other))
    sent.append((xy_in.at[1, last], 9))
    copy(xy_in.at[0, 0], xy_in.at[0, last], 8, at_xy(far, 1, core))
    sent.append((xy_in.at[0, last], 8))
    for k in far_z:
        copy(z_in.at[0], z_in.at[k], 1, at_z(k))
    sent.append((z_in.at[pl.ds(1, NZ - 1)], 1))
    for p in range(last - 1, 0, -1):
        copy(xy_in.at[0, 0], xy_in.at[0, p], 0, at_xy(order[p], 1, core))
    sent.append((xy_in.at[0, near], 0))

    arrived(xy_in.at[0, near], 0)
    copy(xy_in.at[0, pl.ds(0, last)], xy_in.at[1, pl.ds(0, last)], 3, sibling)
    sent.append((xy_in.at[1, pl.ds(0, last)], 3))

    def weigh(image_rows, sign):
        dots = lax.dot_general(image_rows, text_rows, (((1,), (1,)), ((), ())), preferred_element_type=jnp.float32)
        v = sign * (scale * dots + bias)
        small = jnp.exp(-jnp.abs(v))
        losses = jnp.sum(jnp.maximum(v, 0.0) + jnp.log1p(small), axis=1, keepdims=True)
        weights = (sign * jnp.where(v >= 0.0, 1.0, small) / (1.0 + small)).astype(jnp.bfloat16)
        image_grad = scale * jnp.dot(weights, text_rows, preferred_element_type=jnp.float32)
        return losses, weights, image_grad

    def for_texts(weights, image_rows):
        return lax.dot_general(weights, image_rows, (((0,), (0,)), ((), ())), preferred_element_type=jnp.float32)

    def pack_up(p, grad, pieces):
        xy_out[p, :, :D] = grad.astype(jnp.bfloat16)
        xy_out[p, :, D:] = pieces.astype(jnp.bfloat16)

    arrived(z_in.at[pl.ds(1, NZ - 1)], 1)
    text_rows = z_in[...].reshape(columns, D)
    arrived(xy_in.at[0, last], 8)
    mine_rows = xy_in[0].reshape(rows, D)
    loss, weights, mine = weigh(mine_rows, sign)
    pack_up(last, mine[rows - PAIR:], split_sum(loss[rows - PAIR:]))
    copy(xy_out.at[last], xy_back.at[last], 10, at_xy(far, -1, core))
    sent.append((xy_out.at[last], 10))
    text_grad = for_texts(weights, mine_rows)

    arrived(xy_in.at[1, last], 9)
    arrived(xy_in.at[1, pl.ds(0, last)], 3)
    their_rows = xy_in[1].reshape(rows, D)
    losses, weights, theirs = weigh(their_rows, 1.0)
    pieces = split_sum(losses)
    pack_up(nxy, theirs[rows - PAIR:], pieces[rows - PAIR:])
    copy(xy_out.at[nxy], xy_back.at[nxy], 11, at_xy(far, -1, other))
    sent.append((xy_out.at[nxy], 11))
    core_out[:, :D] = theirs.astype(jnp.bfloat16)
    core_out[:, D:] = pieces.astype(jnp.bfloat16)
    copy(core_out, core_in, 5, sibling)
    sent.append((core_out, 5))

    text_grad = scale * (text_grad + for_texts(weights, their_rows))
    for k in far_z:
        z_out[k] = text_grad[k * SLOT:(k + 1) * SLOT].astype(jnp.bfloat16)
        copy(z_out.at[k], z_back.at[k], 6, at_z(-k))
    sent.append((z_out.at[pl.ds(1, NZ - 1)], 6))

    arrived(core_in, 5)
    mine = mine + core_in[:, :D].astype(jnp.float32)
    loss = loss + jnp.sum(core_in[:, D:].astype(jnp.float32), axis=1, keepdims=True)
    pieces = split_sum(loss)
    for p in range(last - 1, 0, -1):
        part = slice(p * PAIR, (p + 1) * PAIR)
        pack_up(p, mine[part], pieces[part])
        copy(xy_out.at[p], xy_back.at[p], 7, at_xy(order[p], -1, core))
    sent.append((xy_out.at[near], 7))

    text_mine = text_grad[:SLOT]
    arrived(z_back.at[pl.ds(1, NZ - 1)], 6)
    for k in range(1, NZ):
        text_mine = text_mine + z_back[k].astype(jnp.float32)
    gc_ref[...] = jnp.where(filled, unnormalize(text_unit, text_inv, text_mine), 0.0)

    arrived(xy_back.at[last], 10)
    arrived(xy_back.at[nxy], 11)
    arrived(xy_back.at[near], 7)
    total = xy_back[1].astype(jnp.float32)
    for p in range(2, nxy + 1):
        total = total + xy_back[p].astype(jnp.float32)
    gi_ref[...] = unnormalize(image_unit, image_inv, mine[:PAIR] + total[:, :D])
    loss = loss[:PAIR] + jnp.sum(total[:, D:], axis=1, keepdims=True)
    loss_ref[...] = (loss / all_pairs - softplus(bias))[:, 0]

    for ref, sem in sent:
        pltpu.make_async_copy(ref, ref, send.at[sem]).wait()


def hand_over(loss_in, gi_in, gc_in, loss_ref, gi_ref, gc_ref):
    loss_ref[...] = loss_in[...]
    gi_ref[...] = gi_in[...]
    gc_ref[...] = gc_in[...]


def body(images, captions, caption_owner, caption_count, log_scale, bias):
    D = images.shape[1]
    W = D + EXTRA
    ny = Y_HI * Y_LO
    nxy = NX * ny
    rows = PAIR * nxy
    all_pairs = PAIR * 2 * NX * ny * NZ
    vmem = pl.BlockSpec(memory_space=pltpu.VMEM)
    half = jnp.bfloat16
    loss, gi, gc = pl.pallas_call(
        functools.partial(kernel, all_pairs),
        out_shape=(
            jax.ShapeDtypeStruct((PAIR,), jnp.float32),
            jax.ShapeDtypeStruct((PAIR, D), jnp.float32),
            jax.ShapeDtypeStruct((SLOT, D), jnp.float32),
        ),
        in_specs=[pl.BlockSpec(memory_space=pltpu.HBM)] * 3 + [pl.BlockSpec(memory_space=pltpu.SMEM)] * 3,
        out_specs=(vmem, vmem, vmem),
        scratch_shapes=[
            pltpu.VMEM((PAIR, D), half),
            pltpu.VMEM((SLOT, D), half),
            pltpu.SMEM((SLOT,), jnp.int32),
            pltpu.VMEM((2, nxy, PAIR, D), half),
            pltpu.VMEM((NZ, SLOT, D), half),
            pltpu.VMEM((rows, W), half),
            pltpu.VMEM((rows, W), half),
            pltpu.VMEM((nxy + 1, PAIR, W), half),
            pltpu.VMEM((nxy + 1, PAIR, W), half),
            pltpu.VMEM((NZ, SLOT, D), half),
            pltpu.VMEM((NZ, SLOT, D), half),
            pltpu.SemaphoreType.DMA((3,)),
            pltpu.SemaphoreType.DMA((12,)),
            pltpu.SemaphoreType.DMA((12,)),
        ],
        compiler_params=pltpu.CompilerParams(
            collective_id=0, has_side_effects=True, vmem_limit_bytes=32 * 1024 * 1024
        ),
    )(
        *[pltpu.with_memory_space_constraint(a, pltpu.HBM) for a in (images, captions, caption_owner)],
        caption_count, log_scale, bias,
    )
    loss, gi, gc = pl.pallas_call(
        hand_over,
        out_shape=(
            jax.ShapeDtypeStruct((PAIR,), jnp.float32),
            jax.ShapeDtypeStruct((PAIR, D), jnp.float32),
            jax.ShapeDtypeStruct((SLOT, D), jnp.float32),
        ),
        in_specs=[vmem] * 3,
        out_specs=(vmem, vmem, vmem),
    )(loss, gi, gc)
    return loss, gi, gc


def solution(mesh):
    placed = (
        P(("dp", "pack"), None),
        P(("dp", "pack"), None),
        P(("dp", "pack")),
        P(("dp", "pack")),
        P(),
        P(),
    )
    return jax.shard_map(
        body,
        mesh=mesh,
        in_specs=placed,
        out_specs=(P(("dp", "pack")), P(("dp", "pack"), None), P(("dp", "pack"), None)),
        check_vma=False,
    )
```

time: 41.3 us -> 41.4 us (level)
  no operation moved by 1% of the time
where the time goes in v3:
time: 41.4 us; the launch traced here: 41.1 us
  Pallas kernels  36.8 us (89%)
  between operations  2.59 us (6%)
  local copies, waits for them, and re-layouts  1.77 us (4%)
    pallas_call x1, Pallas kernels, body(): pl.pallas_call(functools.partial(kernel, all_pairs), out_shape=(jax.Shape...  35.4 us
    unnamed x6, local copies, waits for them, and re-layouts  1.77 us
    pallas_call x1, Pallas kernels, body(): pl.pallas_call(hand_over, out_shape=(jax.ShapeDtypeStruct((PAIR,), jnp.fl...  1.36 us

profile of v3, /device:TPU:1, one launch (start us, length us, event | category | flops | bytes accessed | tf_op | source)
XLA Modules:
  0.0 41.1 jit_solution(11360313431470602140)
XLA Ops:
  2.6 35.4 %shard_map.85 = (f32[2]{0:T(128)S(1)}, f32[2,1152]{1,0:T(2,128)S(1)}, f32[4,1152]{1,0:T(4,128)S(1)}) custom-call(bf16[2,1152]{1,0:T(2,128)(2,1)} %images_hbm.1, bf16[4,1152]{1,0:T(4,128)(2,1)} %captions_hbm.1, s32[4]{0:T(128)} %owner_hbm.1, s32[1]{0:T(128)S(6)} %copy.9.count_ref, f32[1]{0:T(128)S(6)} %copy.10.scale_ref, f32[1]{0:T(128)S(6)} %copy.11.bias_ref), custom_call_target="tpu_custom_call" | custom-call | tf_op jit(solution)/shard_map/pallas_call | solution.py:240
  38.0 0.0 copy-start
  38.0 0.6 %copy-done = f32[4,1152]{1,0:T(4,128)} copy-done((f32[4,1152]{1,0:T(4,128)}, f32[4,1152]{1,0:T(4,128)S(1)}, u32[]{:S(2)}) %copy-start) | copy-done | bytes 18456
  38.6 0.0 copy-start.1
  38.6 0.6 %copy-done.1 = f32[2,1152]{1,0:T(2,128)} copy-done((f32[2,1152]{1,0:T(2,128)}, f32[2,1152]{1,0:T(2,128)S(1)}, u32[]{:S(2)}) %copy-start.1) | copy-done | bytes 9240
  39.2 0.0 copy-start.2
  39.2 0.6 %copy-done.2 = f32[2]{0:T(128)} copy-done((f32[2]{0:T(128)}, f32[2]{0:T(128)S(1)}, u32[]{:S(2)}) %copy-start.2) | copy-done | bytes 32
  39.8 1.4 %shard_map.86 = (f32[2]{0:T(128)}, f32[2,1152]{1,0:T(2,128)}, f32[4,1152]{1,0:T(4,128)}) custom-call(f32[2]{0:T(128)} %copy-done.2, f32[2,1152]{1,0:T(2,128)} %copy-done.1, f32[4,1152]{1,0:T(4,128)} %copy-done), custom_call_target="tpu_custom_call" | custom-call | tf_op jit(solution)/shard_map/pallas_call | solution.py:272
Async XLA Ops:
  38.0 0.6 %copy-start = (f32[4,1152]{1,0:T(4,128)}, f32[4,1152]{1,0:T(4,128)S(1)}, u32[]{:S(2)}) copy-start(f32[4,1152]{1,0:T(4,128)S(1)} %get-tuple-element.8.gc_in) | copy-start | bytes 55300
  38.6 0.6 %copy-start.1 = (f32[2,1152]{1,0:T(2,128)}, f32[2,1152]{1,0:T(2,128)S(1)}, u32[]{:S(2)}) copy-start(f32[2,1152]{1,0:T(2,128)S(1)} %get-tuple-element.7.gi_in) | copy-start | bytes 27652
  39.2 0.6 %copy-start.2 = (f32[2]{0:T(128)}, f32[2]{0:T(128)S(1)}, u32[]{:S(2)}) copy-start(f32[2]{0:T(128)S(1)} %get-tuple-element.6.loss_in) | copy-start | bytes 28

commit v4 on v2

--- a/solution.py
+++ b/solution.py
@@ -120,12 +120,12 @@
     sent.append((xy_in.at[pl.ds(1, nxy - 1)], 0))
 
     arrived(xy_in.at[pl.ds(1, nxy - 1)], 0)
-    x_all[0] = jnp.concatenate([xy_in[k].astype(jnp.float32) for k in range(nxy)], axis=0).astype(jnp.bfloat16)
+    x_all[0] = xy_in[...].reshape(rows, D)
     copy(x_all.at[0], x_all.at[1], 3, sibling)
     sent.append((x_all.at[1], 3))
 
     arrived(z_in.at[pl.ds(1, NZ - 1)], 1)
-    texts[...] = jnp.concatenate([z_in[k].astype(jnp.float32) for k in range(NZ)], axis=0).astype(jnp.bfloat16)
+    texts[...] = z_in[...].reshape(NZ * SLOT, D)
 
     loads[2].wait()
     own = lax.broadcasted_iota(jnp.int32, (2 * rows, NZ * SLOT), 0)
@@ -239,7 +239,7 @@
             pltpu.SemaphoreType.DMA((9,)),
         ],
         compiler_params=pltpu.CompilerParams(
-            collective_id=0, has_side_effects=True, vmem_limit_bytes=32 * 1024 * 1024
+            collective_id=0, has_side_effects=True, vmem_limit_bytes=8 * 1024 * 1024
         ),
     )(
         *[pltpu.with_memory_space_constraint(a, pltpu.HBM) for a in (images, captions, caption_owner)],

time: 41.3 us -> 41.3 us (level)
  no operation moved by 1% of the time
where the time goes in v4:
time: 41.3 us; the launch traced here: 41.1 us
  Pallas kernels  36.7 us (89%)
  between operations  2.59 us (6%)
  local copies, waits for them, and re-layouts  1.77 us (4%)
    pallas_call x1, Pallas kernels, body(): pl.pallas_call(functools.partial(kernel, all_pairs), out_shape=(jax.Shape...  35.4 us
    unnamed x6, local copies, waits for them, and re-layouts  1.77 us
    pallas_call x1, Pallas kernels, body(): pl.pallas_call(hand_over, out_shape=(jax.ShapeDtypeStruct((PAIR,), jnp.fl...  1.36 us

profile of v4, /device:TPU:1, one launch (start us, length us, event | category | flops | bytes accessed | tf_op | source)
XLA Modules:
  0.0 41.1 jit_solution(1509033431485907144)
XLA Ops:
  2.6 35.4 %shard_map.85 = (f32[2]{0:T(128)S(1)}, f32[2,1152]{1,0:T(2,128)S(1)}, f32[4,1152]{1,0:T(4,128)S(1)}) custom-call(bf16[2,1152]{1,0:T(2,128)(2,1)} %images_hbm.1, bf16[4,1152]{1,0:T(4,128)(2,1)} %captions_hbm.1, s32[4]{0:T(128)} %owner_hbm.1, s32[1]{0:T(128)S(6)} %copy.9.count_ref, f32[1]{0:T(128)S(6)} %copy.10.scale_ref, f32[1]{0:T(128)S(6)} %copy.11.bias_ref), custom_call_target="tpu_custom_call" | custom-call | tf_op jit(solution)/shard_map/pallas_call | solution.py:214
  37.9 0.0 copy-start
  37.9 0.6 %copy-done = f32[4,1152]{1,0:T(4,128)} copy-done((f32[4,1152]{1,0:T(4,128)}, f32[4,1152]{1,0:T(4,128)S(1)}, u32[]{:S(2)}) %copy-start) | copy-done | bytes 18456
  38.5 0.0 copy-start.1
  38.5 0.6 %copy-done.1 = f32[2,1152]{1,0:T(2,128)} copy-done((f32[2,1152]{1,0:T(2,128)}, f32[2,1152]{1,0:T(2,128)S(1)}, u32[]{:S(2)}) %copy-start.1) | copy-done | bytes 9240
  39.1 0.0 copy-start.2
  39.1 0.6 %copy-done.2 = f32[2]{0:T(128)} copy-done((f32[2]{0:T(128)}, f32[2]{0:T(128)S(1)}, u32[]{:S(2)}) %copy-start.2) | copy-done | bytes 32
  39.7 1.4 %shard_map.86 = (f32[2]{0:T(128)}, f32[2,1152]{1,0:T(2,128)}, f32[4,1152]{1,0:T(4,128)}) custom-call(f32[2]{0:T(128)} %copy-done.2, f32[2,1152]{1,0:T(2,128)} %copy-done.1, f32[4,1152]{1,0:T(4,128)} %copy-done), custom_call_target="tpu_custom_call" | custom-call | tf_op jit(solution)/shard_map/pallas_call | solution.py:248
Async XLA Ops:
  37.9 0.6 %copy-start = (f32[4,1152]{1,0:T(4,128)}, f32[4,1152]{1,0:T(4,128)S(1)}, u32[]{:S(2)}) copy-start(f32[4,1152]{1,0:T(4,128)S(1)} %get-tuple-element.8.gc_in) | copy-start | bytes 55300
  38.5 0.6 %copy-start.1 = (f32[2,1152]{1,0:T(2,128)}, f32[2,1152]{1,0:T(2,128)S(1)}, u32[]{:S(2)}) copy-start(f32[2,1152]{1,0:T(2,128)S(1)} %get-tuple-element.7.gi_in) | copy-start | bytes 27652
  39.1 0.6 %copy-start.2 = (f32[2]{0:T(128)}, f32[2]{0:T(128)S(1)}, u32[]{:S(2)}) copy-start(f32[2]{0:T(128)S(1)} %get-tuple-element.6.loss_in) | copy-start | bytes 28

commit v5 on v2

v5 whole, which is shorter than its diff:
```python
import functools

import jax
import jax.numpy as jnp
from jax import lax
from jax.experimental import pallas as pl
from jax.experimental.pallas import tpu as pltpu
from jax.sharding import PartitionSpec as P

MESH = pl.DeviceIdType.MESH
EPS = 1e-06
NX, Y_HI, Y_LO, NZ = 4, 2, 4, 12
PAIR, SLOT = 2, 4
EXTRA = 128


def normalize(rows):
    inverse = lax.rsqrt(jnp.sum(rows * rows, axis=-1, keepdims=True) + EPS)
    return rows * inverse, inverse


def unnormalize(unit, inverse, upstream):
    return inverse * (upstream - unit * jnp.sum(unit * upstream, axis=-1, keepdims=True))


def softplus(v):
    return jnp.maximum(v, 0.0) + jnp.log1p(jnp.exp(-jnp.abs(v)))


def split_sum(total):
    high = total.astype(jnp.bfloat16)
    low = (total - high.astype(jnp.float32)).astype(jnp.bfloat16)
    lane = lax.broadcasted_iota(jnp.int32, (total.shape[0], EXTRA), 1)
    return jnp.where(lane == 0, high.astype(jnp.float32), jnp.where(lane == 1, low.astype(jnp.float32), 0.0))


def kernel(
    all_pairs,
    images_hbm, captions_hbm, owner_hbm, count_ref, scale_ref, bias_ref,
    loss_ref, gi_ref, gc_ref,
    images_ref, captions_ref, owner_ref,
    image_mine, text_mine, mine_info, their_info,
    xy_in, z_in, image_rows, text_rows, xy_out, xy_back, z_out, z_back,
    load, send, recv, ready,
):
    D = images_ref.shape[1]
    ny = Y_HI * Y_LO
    nxy = NX * ny
    rows = PAIR * nxy
    columns = SLOT * NZ
    dp = lax.axis_index("dp")
    pack = lax.axis_index("pack")
    core = lax.rem(dp, 2)
    z = lax.rem(dp // 2, NZ)
    y_lo = dp // (2 * NZ)
    x = pack // Y_HI
    y_hi = lax.rem(pack, Y_HI)
    y = y_hi * Y_LO + y_lo

    def device(xx, yy, zz, cc):
        return ((lax.rem(yy, Y_LO) * NZ + zz) * 2 + cc, xx * Y_HI + yy // Y_LO)

    def at_xy(k, way, cc):
        kx, ky = k % NX, k // NX
        return device(lax.rem(x + way * kx + NX, NX), lax.rem(y + way * ky + ny, ny), z, cc)

    def at_z(k, way, cc):
        return device(x, y, lax.rem(z + way * k + NZ, NZ), cc)

    sibling = device(x, y, z, 1 - core)

    def hops(k, n):
        return min(k, n - k)

    far_xy = sorted(range(1, nxy), key=lambda k: -hops(k % NX, NX) - hops(k // NX, ny))
    far_z = sorted(range(1, NZ), key=lambda k: -hops(k, NZ))

    barrier = pltpu.get_barrier_semaphore()

    def greet(partner):
        pl.semaphore_signal(barrier, inc=1, device_id=partner, device_id_type=MESH)

    greet(sibling)

    @pl.when(core == 0)
    def _():
        for k in far_z:
            greet(at_z(k, 1, 0))

    @pl.when(core == 1)
    def _():
        for k in far_xy:
            greet(at_xy(k, 1, 1))

    loads = [
        pltpu.make_async_copy(src, dst, load.at[i])
        for i, (src, dst) in enumerate((
            (images_hbm, images_ref), (captions_hbm, captions_ref), (owner_hbm, owner_ref),
        ))
    ]
    for one in loads:
        one.start()
    loads[0].wait()
    image_unit, image_inv = normalize(images_ref[...].astype(jnp.float32))
    image_mine[0] = image_unit.astype(jnp.bfloat16)
    loads[1].wait()
    slot_row = lax.broadcasted_iota(jnp.int32, (SLOT, 1), 0)
    filled = slot_row < count_ref[0]
    captions = jnp.where(filled, captions_ref[...].astype(jnp.float32), 0.0)
    text_unit, text_inv = normalize(captions)
    text_mine[0] = text_unit.astype(jnp.bfloat16)
    loads[2].wait()
    lane = lax.broadcasted_iota(jnp.int32, mine_info.shape, 1)
    info = jnp.full(mine_info.shape, -2, jnp.int32)
    for s in range(SLOT):
        info = jnp.where(jnp.logical_and(lane == core * columns + s, s < count_ref[0]), owner_ref[s], info)
    mine_info[...] = info

    def copy(src, dst, sem, to):
        pltpu.make_async_remote_copy(
            src_ref=src, dst_ref=dst, send_sem=send.at[sem], recv_sem=recv.at[sem],
            device_id=to, device_id_type=MESH,
        ).start()

    def arrived(ref, sem):
        pltpu.make_async_copy(ref, ref, recv.at[sem]).wait()

    def left(ref, sem):
        pltpu.make_async_copy(ref, ref, send.at[sem]).wait()

    def announce():
        pl.semaphore_signal(ready.at[0], inc=1, device_id=sibling, device_id_type=MESH)

    def send_images(slot):
        for k in far_xy:
            copy(image_mine.at[0], xy_in.at[slot + k], 0, at_xy(k, 1, 1))

    def send_texts(slot):
        for k in far_z:
            copy(text_mine.at[0], z_in.at[slot + k], 1, at_z(k, 1, 0))

    @pl.when(core == 0)
    def _():
        pl.semaphore_wait(barrier, NZ)
        announce()
        send_texts(0)
        copy(mine_info, their_info, 2, sibling)
        copy(image_mine.at[0], xy_in.at[nxy], 0, sibling)
        z_in[0] = text_mine[0]
        pl.semaphore_wait(ready.at[0], 1)
        send_images(nxy)
        arrived(z_in.at[pl.ds(1, 2 * NZ - 1)], 1)
        text_rows[...] = z_in[...].reshape(2 * columns, D)
        copy(text_rows, text_rows, 4, sibling)

    @pl.when(core == 1)
    def _():
        pl.semaphore_wait(barrier, nxy)
        announce()
        send_images(0)
        copy(mine_info, their_info, 2, sibling)
        copy(text_mine.at[0], z_in.at[NZ], 1, sibling)
        xy_in[0] = image_mine[0]
        pl.semaphore_wait(ready.at[0], 1)
        send_texts(NZ)
        arrived(xy_in.at[pl.ds(1, 2 * nxy - 1)], 0)
        image_rows[...] = xy_in[...].reshape(2 * rows, D)
        copy(image_rows, image_rows, 3, sibling)

    own = lax.broadcasted_iota(jnp.int32, (2 * rows, 2 * columns), 0)
    column = lax.broadcasted_iota(jnp.int32, (2 * rows, 2 * columns), 1)
    slot = lax.rem(own, rows) // PAIR
    y_slot = slot // NX
    from_x = lax.rem(x - lax.rem(slot, NX) + NX, NX)
    from_y_hi = lax.rem(y_hi - y_slot // Y_LO + Y_HI, Y_HI)
    pair = (from_x * Y_HI + from_y_hi) * PAIR + lax.rem(own, PAIR)
    same = jnp.logical_and(1 - own // rows == column // columns, lax.rem(y_slot, Y_LO) == 0)
    pair = jnp.where(same, pair, -1)
    scale = jnp.exp(jnp.full((1, 1), scale_ref[0], jnp.float32))
    bias = jnp.full((1, 1), bias_ref[0], jnp.float32)
    arrived(their_info, 2)
    owner = jnp.maximum(mine_info[...], their_info[...])[:1, :2 * columns]
    sign = jnp.where(pair == owner, -1.0, 1.0)

    @pl.when(core == 0)
    def _():
        arrived(image_rows, 3)

    @pl.when(core == 1)
    def _():
        arrived(text_rows, 4)

    dots = lax.dot_general(
        image_rows[...], text_rows[...], (((1,), (1,)), ((), ())), preferred_element_type=jnp.float32
    )
    v = sign * (scale * dots + bias)
    small = jnp.exp(-jnp.abs(v))
    weights = (sign * jnp.where(v >= 0.0, 1.0, small) / (1.0 + small)).astype(jnp.bfloat16)

    @pl.when(core == 0)
    def _():
        grad = scale * lax.dot_general(
            weights, image_rows[...], (((0,), (0,)), ((), ())), preferred_element_type=jnp.float32
        )
        z_out[...] = grad.astype(jnp.bfloat16).reshape(2 * NZ, SLOT, D)
        for k in far_z:
            copy(z_out.at[k], z_back.at[k], 5, at_z(k, -1, 0))
            copy(z_out.at[NZ + k], z_back.at[k], 5, at_z(k, -1, 1))
        copy(z_out.at[NZ], z_back.at[0], 5, sibling)
        z_back[0] = z_out[0]
        arrived(z_back.at[pl.ds(1, NZ - 1)], 5)

    @pl.when(core == 1)
    def _():
        losses = jnp.sum(jnp.maximum(v, 0.0) + jnp.log1p(small), axis=1, keepdims=True)
        grad = scale * jnp.dot(weights, text_rows[...], preferred_element_type=jnp.float32)
        xy_out[:, :, :D] = grad.astype(jnp.bfloat16).reshape(2 * nxy, PAIR, D)
        xy_out[:, :, D:] = split_sum(losses).astype(jnp.bfloat16).reshape(2 * nxy, PAIR, EXTRA)
        for k in far_xy:
            copy(xy_out.at[k], xy_back.at[k], 6, at_xy(k, -1, 1))
            copy(xy_out.at[nxy + k], xy_back.at[k], 6, at_xy(k, -1, 0))
        copy(xy_out.at[nxy], xy_back.at[0], 6, sibling)
        xy_back[0] = xy_out[0]
        arrived(z_back, 5)

    text_grad = z_back[0].astype(jnp.float32)
    for k in range(1, NZ):
        text_grad = text_grad + z_back[k].astype(jnp.float32)
    gc_ref[...] = jnp.where(filled, unnormalize(text_unit, text_inv, text_grad), 0.0)

    @pl.when(core == 0)
    def _():
        arrived(xy_back, 6)

    @pl.when(core == 1)
    def _():
        arrived(xy_back.at[pl.ds(1, nxy - 1)], 6)

    total = xy_back[0].astype(jnp.float32)
    for k in range(1, nxy):
        total = total + xy_back[k].astype(jnp.float32)
    gi_ref[...] = unnormalize(image_unit, image_inv, total[:, :D])
    loss = jnp.sum(total[:, D:], axis=1, keepdims=True)
    loss_ref[...] = (loss / all_pairs - softplus(bias))[:, 0]

    left(mine_info, 2)

    @pl.when(core == 0)
    def _():
        left(xy_in.at[pl.ds(0, nxy)], 0)
        left(z_in.at[pl.ds(0, NZ - 1)], 1)
        left(text_rows, 4)
        left(z_out.at[pl.ds(0, 2 * NZ - 1)], 5)

    @pl.when(core == 1)
    def _():
        left(xy_in.at[pl.ds(0, nxy - 1)], 0)
        left(z_in.at[pl.ds(0, NZ)], 1)
        left(image_rows, 3)
        left(xy_out.at[pl.ds(0, 2 * nxy - 1)], 6)


def hand_over(loss_in, gi_in, gc_in, loss_ref, gi_ref, gc_ref):
    loss_ref[...] = loss_in[...]
    gi_ref[...] = gi_in[...]
    gc_ref[...] = gc_in[...]


def body(images, captions, caption_owner, caption_count, log_scale, bias):
    D = images.shape[1]
    W = D + EXTRA
    ny = Y_HI * Y_LO
    nxy = NX * ny
    rows = PAIR * nxy
    all_pairs = PAIR * 2 * NX * ny * NZ
    vmem = pl.BlockSpec(memory_space=pltpu.VMEM)
    half = jnp.bfloat16
    loss, gi, gc = pl.pallas_call(
        functools.partial(kernel, all_pairs),
        out_shape=(
            jax.ShapeDtypeStruct((PAIR,), jnp.float32),
            jax.ShapeDtypeStruct((PAIR, D), jnp.float32),
            jax.ShapeDtypeStruct((SLOT, D), jnp.float32),
        ),
        in_specs=[pl.BlockSpec(memory_space=pltpu.HBM)] * 3 + [pl.BlockSpec(memory_space=pltpu.SMEM)] * 3,
        out_specs=(vmem, vmem, vmem),
        scratch_shapes=[
            pltpu.VMEM((PAIR, D), half),
            pltpu.VMEM((SLOT, D), half),
            pltpu.SMEM((SLOT,), jnp.int32),
            pltpu.VMEM((1, PAIR, D), half),
            pltpu.VMEM((1, SLOT, D), half),
            pltpu.VMEM((8, 128), jnp.int32),
            pltpu.VMEM((8, 128), jnp.int32),
            pltpu.VMEM((2 * nxy, PAIR, D), half),
            pltpu.VMEM((2 * NZ, SLOT, D), half),
            pltpu.VMEM((2 * rows, D), half),
            pltpu.VMEM((2 * NZ * SLOT, D), half),
            pltpu.VMEM((2 * nxy, PAIR, W), half),
            pltpu.VMEM((nxy, PAIR, W), half),
            pltpu.VMEM((2 * NZ, SLOT, D), half),
            pltpu.VMEM((NZ, SLOT, D), half),
            pltpu.SemaphoreType.DMA((3,)),
            pltpu.SemaphoreType.DMA((7,)),
            pltpu.SemaphoreType.DMA((7,)),
            pltpu.SemaphoreType.REGULAR((1,)),
        ],
        compiler_params=pltpu.CompilerParams(
            collective_id=0, has_side_effects=True, vmem_limit_bytes=32 * 1024 * 1024
        ),
    )(
        *[pltpu.with_memory_space_constraint(a, pltpu.HBM) for a in (images, captions, caption_owner)],
        caption_count, log_scale, bias,
    )
    loss, gi, gc = pl.pallas_call(
        hand_over,
        out_shape=(
            jax.ShapeDtypeStruct((PAIR,), jnp.float32),
            jax.ShapeDtypeStruct((PAIR, D), jnp.float32),
            jax.ShapeDtypeStruct((SLOT, D), jnp.float32),
        ),
        in_specs=[vmem] * 3,
        out_specs=(vmem, vmem, vmem),
    )(loss, gi, gc)
    return loss, gi, gc


def solution(mesh):
    placed = (
        P(("dp", "pack"), None),
        P(("dp", "pack"), None),
        P(("dp", "pack")),
        P(("dp", "pack")),
        P(),
        P(),
    )
    return jax.shard_map(
        body,
        mesh=mesh,
        in_specs=placed,
        out_specs=(P(("dp", "pack")), P(("dp", "pack"), None), P(("dp", "pack"), None)),
        check_vma=False,
    )
```

time: 41.3 us -> 41.7 us (level)
  no operation moved by 1% of the time
where the time goes in v5:
time: 41.7 us; the launch traced here: 41.5 us
  Pallas kernels  37.1 us (89%)
  between operations  2.59 us (6%)
  local copies, waits for them, and re-layouts  1.77 us (4%)
    pallas_call x1, Pallas kernels, body(): pl.pallas_call(functools.partial(kernel, all_pairs), out_shape=(jax.Shape...  35.7 us
    unnamed x6, local copies, waits for them, and re-layouts  1.77 us
    pallas_call x1, Pallas kernels, body(): pl.pallas_call(hand_over, out_shape=(jax.ShapeDtypeStruct((PAIR,), jnp.fl...  1.36 us

profile of v5, /device:TPU:1, one launch (start us, length us, event | category | flops | bytes accessed | tf_op | source)
XLA Modules:
  0.0 41.5 jit_solution(14759577287651270256)
XLA Ops:
  2.6 35.7 %shard_map.85 = (f32[2]{0:T(128)S(1)}, f32[2,1152]{1,0:T(2,128)S(1)}, f32[4,1152]{1,0:T(4,128)S(1)}) custom-call(bf16[2,1152]{1,0:T(2,128)(2,1)} %images_hbm.1, bf16[4,1152]{1,0:T(4,128)(2,1)} %captions_hbm.1, s32[4]{0:T(128)} %owner_hbm.1, s32[1]{0:T(128)S(6)} %copy.9.count_ref, f32[1]{0:T(128)S(6)} %copy.10.scale_ref, f32[1]{0:T(128)S(6)} %copy.11.bias_ref), custom_call_target="tpu_custom_call" | custom-call | tf_op jit(solution)/shard_map/pallas_call | solution.py:278
  38.3 0.0 copy-start
  38.3 0.6 %copy-done = f32[4,1152]{1,0:T(4,128)} copy-done((f32[4,1152]{1,0:T(4,128)}, f32[4,1152]{1,0:T(4,128)S(1)}, u32[]{:S(2)}) %copy-start) | copy-done | bytes 18456
  38.9 0.0 copy-start.1
  38.9 0.6 %copy-done.1 = f32[2,1152]{1,0:T(2,128)} copy-done((f32[2,1152]{1,0:T(2,128)}, f32[2,1152]{1,0:T(2,128)S(1)}, u32[]{:S(2)}) %copy-start.1) | copy-done | bytes 9240
  39.5 0.0 copy-start.2
  39.5 0.6 %copy-done.2 = f32[2]{0:T(128)} copy-done((f32[2]{0:T(128)}, f32[2]{0:T(128)S(1)}, u32[]{:S(2)}) %copy-start.2) | copy-done | bytes 32
  40.1 1.4 %shard_map.86 = (f32[2]{0:T(128)}, f32[2,1152]{1,0:T(2,128)}, f32[4,1152]{1,0:T(4,128)}) custom-call(f32[2]{0:T(128)} %copy-done.2, f32[2,1152]{1,0:T(2,128)} %copy-done.1, f32[4,1152]{1,0:T(4,128)} %copy-done), custom_call_target="tpu_custom_call" | custom-call | tf_op jit(solution)/shard_map/pallas_call | solution.py:315
Async XLA Ops:
  38.3 0.6 %copy-start = (f32[4,1152]{1,0:T(4,128)}, f32[4,1152]{1,0:T(4,128)S(1)}, u32[]{:S(2)}) copy-start(f32[4,1152]{1,0:T(4,128)S(1)} %get-tuple-element.8.gc_in) | copy-start | bytes 55300
  38.9 0.6 %copy-start.1 = (f32[2,1152]{1,0:T(2,128)}, f32[2,1152]{1,0:T(2,128)S(1)}, u32[]{:S(2)}) copy-start(f32[2,1152]{1,0:T(2,128)S(1)} %get-tuple-element.7.gi_in) | copy-start | bytes 27652
  39.5 0.6 %copy-start.2 = (f32[2]{0:T(128)}, f32[2]{0:T(128)S(1)}, u32[]{:S(2)}) copy-start(f32[2]{0:T(128)S(1)} %get-tuple-element.6.loss_in) | copy-start | bytes 28
